TPU v7x, 512 devices: a whole 4x4x16 slice. The times are simulated.
512 devices in a mesh: replica: 32 (over z, core), fsdp: 16 (over y, x).
Axes of the slice: x: 4, y: 4, z: 16, core: 2. Of those that a mesh axis runs over, the one named last changes fastest.
Arguments:
- weights: bfloat16 [3, 32, 28672], P(None, None, 'fsdp'), may hold values from -4 to 4
- local_weights: bfloat16 [32, 3, 32, 28672], P('replica', None, None, 'fsdp'), may hold values from -11 to 11
- carried_error: float32 [32, 3, 32, 28672], P('replica', None, None, 'fsdp'), may hold values from -4 to 4
- momentum: float32 [3, 32, 28672], P(None, None, 'fsdp'), may hold values from -4 to 4
- initial_factor: float32 [3, 32, 16], replicated, may hold values from -5 to 5
Outputs:
- next_weights: bfloat16 [3, 32, 28672], P(None, None, 'fsdp')
- next_error: float32 [32, 3, 32, 28672], P('replica', None, None, 'fsdp')
- next_momentum: float32 [3, 32, 28672], P(None, None, 'fsdp')
- following_factor: float32 [3, 32, 16], replicated
All inputs are finite; a program needn't handle non-finite values.
Results may differ from a plain program's by a relative error of at most 0.001.
Values sent between devices are 32-bit elements; how exact they have to be, the bound alone decides.
No kernel may reach another device: no remote copies, remote signals or barrier semaphores. Data moves between devices by JAX's collectives and lax.ppermute only.
A program may use at most 64 MiB of HBM per device.

v0:
```python
import jax
import jax.numpy as jnp
from jax import lax
from jax.experimental import pallas as pl
from jax.experimental.pallas import tpu as pltpu
from jax.sharding import PartitionSpec as P

CHIPS = 16
BLOCK = 128
SIDE = BLOCK // 2
BLOCKS = 14
WIDTH = BLOCK * BLOCKS
MATS = 3
COLS = 32
RANK = 16
SHARE = MATS * COLS // 2
FROWS = SHARE // 2
MROWS = 8
GROWS = FROWS + MROWS
PAIR = RANK + COLS
HIGHEST = lax.Precision.HIGHEST
VMEM = pl.BlockSpec(memory_space=pltpu.VMEM)
SMEM = pl.BlockSpec(memory_space=pltpu.SMEM)
HBM = pl.BlockSpec(memory_space=pl.ANY)
PARAMS = pltpu.CompilerParams(vmem_limit_bytes=32 * 1024 * 1024)
PACK_PARAMS = pltpu.CompilerParams(vmem_limit_bytes=56 * 1024 * 1024)


REVERSED = [int(format(i, "04b")[::-1], 2) for i in range(CHIPS)]


def slot_of(chip, core):
    return REVERSED[chip] ^ (3 * core)


def chip_at(slot, core):
    return REVERSED[slot ^ (3 * core)]


def swap_sides(x):
    return pltpu.roll(x, SIDE, 1)


def left_side(rows):
    return lax.broadcasted_iota(jnp.int32, (rows, BLOCK), 1) < SIDE


def pack_kernel(ids, w_hbm, lw_hbm, ce_hbm, keep, send, drift, w, lw, ce, sems):
    core = ids[0]
    copies = [
        [
            pltpu.make_async_copy(src.at[mat], dst.at[mat], sems.at[kind, mat])
            for kind, (src, dst) in enumerate(((ce_hbm, ce), (w_hbm, w), (lw_hbm, lw)))
        ]
        for mat in range(MATS)
    ]
    for group in copies:
        for copy in group:
            copy.start()
    left = left_side(16)
    for block in range(BLOCKS, CHIPS):
        keep[slot_of(block, core)] = jnp.zeros((SHARE, BLOCK), jnp.float32)
        send[slot_of(block, 1 - core)] = jnp.zeros((SHARE, BLOCK), jnp.float32)
    for mat in range(MATS):
        for copy in copies[mat]:
            copy.wait()
        for block in range(BLOCKS):
            lanes = slice(block * BLOCK, (block + 1) * BLOCK)
            value = (
                w[mat, :, lanes].astype(jnp.float32)
                - lw[mat, :, lanes].astype(jnp.float32)
                + ce[mat, :, lanes]
            )
            drift[mat, :, lanes] = value
    for block in range(BLOCKS):
        lanes = slice(block * BLOCK, (block + 1) * BLOCK)
        keep[slot_of(block, core), 0:COLS] = drift[2 * core, :, lanes]
        send[slot_of(block, 1 - core), 0:COLS] = drift[2 - 2 * core, :, lanes]
        top, bottom = drift[1, 0:16, lanes], drift[1, 16:32, lanes]
        first = jnp.where(left, top, swap_sides(bottom))
        second = jnp.where(left, swap_sides(top), bottom)
        keep[slot_of(block, core), COLS:SHARE] = jnp.where(core == 0, first, second)
        send[slot_of(block, 1 - core), COLS:SHARE] = jnp.where(core == 0, second, first)


def outer(a, b):
    return lax.dot_general(
        a, b, (((1,), (1,)), ((), ())), precision=HIGHEST, preferred_element_type=jnp.float32
    )


def factor_kernel(ids, qt, got, inner, factor):
    core = ids[0]
    total = jnp.sum(got[...], axis=0)
    left = left_side(16)
    whole = total[0:COLS]
    half = total[COLS:SHARE]
    half = jnp.concatenate(
        [jnp.where(left, half, 0.0), jnp.where(left, swap_sides(half), 0.0)], axis=0
    )
    whole_factor = jnp.dot(
        qt[2 * core], whole, precision=HIGHEST, preferred_element_type=jnp.float32
    )
    half_factor = jnp.dot(qt[1], half, precision=HIGHEST, preferred_element_type=jnp.float32)
    factor[0:RANK] = whole_factor
    factor[RANK:FROWS] = half_factor[0:8] + swap_sides(half_factor[8:16])
    whole, half = outer(whole_factor, whole), outer(half_factor, half)
    inner[...] = jnp.concatenate([whole[0:8], whole[8:16], half[0:8], half[8:16]], axis=1)


def split(x):
    high = x.astype(jnp.bfloat16)
    rest = x - high.astype(jnp.float32)
    middle = rest.astype(jnp.bfloat16)
    return high, middle, (rest - middle.astype(jnp.float32)).astype(jnp.bfloat16)


def final_kernel(
    islands, ids, qt, own, sib, w, mom, drift,
    out_w, out_e, out_m, out_f, fac, buf_w, buf_e, buf_m, sems,
):
    first = ids[0] == 0

    mine = jnp.sum(own[:, FROWS:GROWS], axis=0)
    other = jnp.sum(sib[:, FROWS:GROWS], axis=0)
    middle = pltpu.roll(mine + other, SIDE, 1)
    table = []
    for mat, rows in enumerate(
        (jnp.where(first, mine, other), middle, jnp.where(first, other, mine))
    ):
        rows = jnp.concatenate([rows[:, 0:COLS], rows[:, COLS : 2 * COLS]], axis=0)
        gram = outer(qt[mat], rows)
        rest = jnp.zeros((RANK, BLOCK - PAIR), jnp.float32)
        table.append(jnp.concatenate([gram, rows, rest], axis=1))
    table = jnp.stack(table)
    row = lax.broadcasted_iota(jnp.int32, table.shape, 1)
    small = table
    for step in range(RANK):
        spread = jnp.broadcast_to(table[:, :, step : step + 1], table.shape)
        pivot = spread[:, step : step + 1, :]
        line = table[:, step : step + 1, :]
        scaled = line * (1.0 / pivot)
        here = row == step
        small = jnp.where(here, line * lax.rsqrt(pivot), small)
        table = jnp.where(here, scaled, table - spread * scaled)

    left = left_side(8)
    for block in range(BLOCKS):
        lanes = slice(block * BLOCK, (block + 1) * BLOCK)
        mine = own[slot_of(block, ids[0]), 0:FROWS]
        other = sib[slot_of(block, 1 - ids[0]), 0:FROWS]
        low, high = jnp.where(first, mine, other), jnp.where(first, other, mine)
        low_half, high_half = low[RANK:FROWS], high[RANK:FROWS]
        half = jnp.concatenate(
            [
                jnp.where(left, low_half, swap_sides(high_half)),
                jnp.where(left, swap_sides(low_half), high_half),
            ],
            axis=0,
        )
        for mat, value in enumerate((low[0:RANK], half, high[0:RANK])):
            top, mid, last = split(value)
            for place, part in enumerate((top, mid, last, top, mid, top)):
                fac[mat, place * RANK : place * RANK + RANK, lanes] = part

    for mat in range(MATS):
        out_f[mat] = small[mat, :, RANK:PAIR] * (1.0 / islands)
        top, mid, last = split(table[mat, :, RANK:PAIR] * (1.0 / islands))
        parts = [x.astype(jnp.float32) for x in (top, top, top, mid, mid, last)]
        mixed = jnp.transpose(jnp.concatenate(parts, axis=0)).astype(jnp.bfloat16)
        for tile in range(7):
            lanes = slice(tile * 256, (tile + 1) * 256)
            approx = jnp.dot(mixed, fac[mat, :, lanes], preferred_element_type=jnp.float32)
            wide = w[mat, :, lanes].astype(jnp.float32)
            momentum = 0.9 * mom[mat, :, lanes] + approx
            buf_e[mat, :, lanes] = drift[mat, :, lanes] - approx
            buf_m[mat, :, lanes] = momentum
            buf_w[mat, :, lanes] = (wide - 0.7 * (approx + 0.9 * momentum)).astype(jnp.bfloat16)
        for kind, (buf, out) in enumerate(((buf_w, out_w), (buf_e, out_e), (buf_m, out_m))):
            pltpu.make_async_copy(buf.at[mat], out.at[mat], sems.at[kind, mat]).start()
    for mat in range(MATS):
        for kind, (buf, out) in enumerate(((buf_w, out_w), (buf_e, out_e), (buf_m, out_m))):
            pltpu.make_async_copy(buf.at[mat], out.at[mat], sems.at[kind, mat]).wait()


def sibling(x):
    return lax.ppermute(x, "replica", [(i, i ^ 1) for i in range(2 * CHIPS)])


def exchange_z(x):
    groups = [[2 * chip_at(slot, core) + core for slot in range(CHIPS)] for core in range(2)]
    return lax.all_to_all(x, "replica", 0, 0, axis_index_groups=groups, tiled=True)


def local(weights, local_weights, carried_error, momentum, initial_factor):
    f32 = jnp.float32
    ids = (lax.axis_index("replica") & 1).astype(jnp.int32).reshape(1)
    shape = (MATS, COLS, WIDTH)
    keep, send, drift = pl.pallas_call(
        pack_kernel,
        out_shape=[pltpu.VMEM((CHIPS, SHARE, BLOCK), f32)] * 2 + [pltpu.VMEM(shape, f32)],
        in_specs=[SMEM, HBM, HBM, HBM],
        out_specs=[VMEM] * 3,
        scratch_shapes=[
            pltpu.VMEM(shape, jnp.bfloat16),
            pltpu.VMEM(shape, jnp.bfloat16),
            pltpu.VMEM(shape, f32),
            pltpu.SemaphoreType.DMA((3, 3)),
        ],
        compiler_params=PACK_PARAMS,
        name="pack",
    )(ids, weights, local_weights[0], carried_error[0])
    qt = jnp.swapaxes(initial_factor, 1, 2)
    shares = exchange_z(keep + sibling(send))
    inner, factor = pl.pallas_call(
        factor_kernel,
        out_shape=[
            jax.ShapeDtypeStruct((MROWS, BLOCK), f32),
            jax.ShapeDtypeStruct((FROWS, BLOCK), f32),
        ],
        in_specs=[SMEM, VMEM, VMEM],
        out_specs=[VMEM, VMEM],
        compiler_params=PARAMS,
        name="factor",
    )(ids, qt, shares)

    inner = lax.all_to_all(
        jnp.broadcast_to(inner, (16, MROWS, BLOCK)), "fsdp", 0, 0, tiled=True
    )
    inner = jnp.sum(inner, axis=0)
    own = exchange_z(
        jnp.broadcast_to(jnp.concatenate([factor, inner]), (CHIPS, GROWS, BLOCK))
    )
    sib = sibling(own)

    next_weights, next_error, next_momentum, following = pl.pallas_call(
        lambda *refs: final_kernel(lax.axis_size("replica"), *refs),
        out_shape=[
            jax.ShapeDtypeStruct(shape, jnp.bfloat16),
            jax.ShapeDtypeStruct(shape, f32),
            jax.ShapeDtypeStruct(shape, f32),
            jax.ShapeDtypeStruct((MATS, RANK, COLS), f32),
        ],
        in_specs=[SMEM] + [VMEM] * 6,
        out_specs=[HBM, HBM, HBM, VMEM],
        scratch_shapes=[
            pltpu.VMEM((MATS, 6 * RANK, WIDTH), jnp.bfloat16),
            pltpu.VMEM(shape, jnp.bfloat16),
            pltpu.VMEM(shape, f32),
            pltpu.VMEM(shape, f32),
            pltpu.SemaphoreType.DMA((3, 3)),
        ],
        compiler_params=PARAMS,
        name="final",
    )(ids, qt, own, sib, weights, momentum, drift)
    return (next_weights, next_error[None], next_momentum, jnp.swapaxes(following, 1, 2))


def solution(mesh):
    return jax.shard_map(
        local,
        mesh=mesh,
        in_specs=(
            P(None, None, "fsdp"),
            P("replica", None, None, "fsdp"),
            P("replica", None, None, "fsdp"),
            P(None, None, "fsdp"),
            P(),
        ),
        out_specs=(
            P(None, None, "fsdp"),
            P("replica", None, None, "fsdp"),
            P(None, None, "fsdp"),
            P(),
        ),
        check_vma=False,
    )
```

profile of v0, /device:TPU:1, one launch (start us, length us, event | category | flops | bytes accessed | tf_op | source)
XLA Modules:
  0.0 91.5 jit_solution(11800560068808033046)
XLA Ops:
  0.6 1.6 %pack.1 = (f32[16,48,128]{2,1,0:T(8,128)S(1)}, f32[16,48,128]{2,1,0:T(8,128)S(1)}, f32[3,32,1792]{2,1,0:T(8,128)S(1)}) custom-call(s32[1]{0:T(128)} %bitcast.ids.refs_0_, bf16[3,32,1792]{2,1,0:T(8,128)(2,1)} %refs_4_.1, bf16[3,32,1792]{2,1,0:T(8,128)(2,1)} %bitcast.9, f32[3,32,1792]{2,1,0:T(8,128)} %bitcast.8), custom_call_target="tpu_custom_call" | custom-call | tf_op jit(solution)/shard_map/pack/pallas_call | solution.py:199
  2.3 8.8 %collective-permute-start = (f32[16,48,128]{2,1,0:T(8,128)S(1)}, f32[16,48,128]{2,1,0:T(8,128)S(1)}, u32[]{:S(2)}, u32[]{:S(2)}) collective-permute-start(f32[16,48,128]{2,1,0:T(8,128)S(1)} %get-tuple-element.14), channel_id=1, source_target_pairs={{0,16},{16,0},{32,48},{48,32},{64,80},{80,64},{96,112},{112,96},{1... | collective-permute-start | bytes 1179656 | tf_op jit(solution)/shard_map/ppermute | solution.py:187
  11.1 1.3 %collective-permute-done = f32[16,48,128]{2,1,0:T(8,128)S(1)} collective-permute-done((f32[16,48,128]{2,1,0:T(8,128)S(1)}, f32[16,48,128]{2,1,0:T(8,128)S(1)}, u32[]{:S(2)}, u32[]{:S(2)}) %collective-permute-start) | collective-permute-done | bytes 393248 | tf_op jit(solution)/shard_map/ppermute | solution.py:187
  12.4 0.0 copy-start.2
  12.5 32.6 %all_to_all.15.got = f32[16,48,128]{2,1,0:T(8,128)S(1)} all-to-all(f32[16,48,128]{2,1,0:T(8,128)S(1)} %add.3), channel_id=1, replica_groups={{0,256,128,384,64,320,192,448,32,288,160,416,96,352,224,480},{400,144,2..., dimensions={0} | all-to-all | bytes 786432 | tf_op jit(solution)/shard_map/all_to_all | solution.py:192
  45.0 0.0 copy-done.2
  45.0 0.0 copy-start.1
  45.0 0.4 factor.1
  45.5 13.1 %all_to_all.16 = f32[16,8,128]{2,1,0:T(8,128)S(1)} all-to-all(f32[16,8,128]{2,1,0:T(8,128)S(1)} %broadcast_in_dim.9), channel_id=1, replica_groups=mesh['replica'=32,'fsdp'=16] {'fsdp'}, dimensions={0} | all-to-all | bytes 131072 | tf_op jit(solution)/shard_map/all_to_all | solution.py:227
  58.6 0.0 copy-start
  58.6 20.7 %all_to_all.17.refs_2_ = f32[16,32,128]{2,1,0:T(8,128)S(1)} all-to-all(f32[16,32,128]{2,1,0:T(8,128)S(1)} %broadcast_in_dim.10), channel_id=1, replica_groups={{0,256,128,384,64,320,192,448,32,288,160,416,96,352,224,480},{400,144,2..., dimensions={0} | all-to-all | bytes 524288 | tf_op jit(solution)/shard_map/all_to_all | solution.py:192
  79.3 7.2 %collective-permute-start.1 = (f32[16,32,128]{2,1,0:T(8,128)S(1)}, f32[16,32,128]{2,1,0:T(8,128)S(1)}, u32[]{:S(2)}, u32[]{:S(2)}) collective-permute-start(f32[16,32,128]{2,1,0:T(8,128)S(1)} %all_to_all.17.refs_2_), channel_id=1, source_target_pairs={{0,16},{16,0},{32,48},{48,32},{64,80},{80,64},{96,112},{112,96},{1... | collective-permute-start | bytes 786440 | tf_op jit(solution)/shard_map/ppermute | solution.py:187
  86.5 1.1 %collective-permute-done.1.refs_3_ = f32[16,32,128]{2,1,0:T(8,128)S(1)} collective-permute-done((f32[16,32,128]{2,1,0:T(8,128)S(1)}, f32[16,32,128]{2,1,0:T(8,128)S(1)}, u32[]{:S(2)}, u32[]{:S(2)}) %collective-permute-start.1) | collective-permute-done | bytes 262176 | tf_op jit(solution)/shard_map/ppermute | solution.py:187
  87.7 0.0 copy-done.1
  87.7 0.0 copy-done
  87.7 3.8 %final.1 = (bf16[3,32,1792]{2,1,0:T(8,128)(2,1)}, f32[3,32,1792]{2,1,0:T(8,128)}, f32[3,32,1792]{2,1,0:T(8,128)}, f32[3,16,32]{2,1,0:T(8,128)}) custom-call(s32[1]{0:T(128)} %bitcast.ids.refs_0_, f32[3,16,32]{2,1,0:T(8,128)S(1)} %bitcast.7, f32[16,32,128]{2,1,0:T(8,128)S(1)} %all_to_all.17.refs_2_, f32[16,32,128]{2,1,0:T(8,128)S(1)} %collective-permute-done.1.refs_3_, ...), custom_call_target="tpu_custom_call" | custom-call | tf_op jit(solution)/shard_map/final/pallas_call | solution.py:236
  (5 shorter events, 0.1 us)
Async XLA Ops:
  2.3 10.1 %collective-permute-start = (f32[16,48,128]{2,1,0:T(8,128)S(1)}, f32[16,48,128]{2,1,0:T(8,128)S(1)}, u32[]{:S(2)}, u32[]{:S(2)}) collective-permute-start(f32[16,48,128]{2,1,0:T(8,128)S(1)} %get-tuple-element.14), channel_id=1, source_target_pairs={{0,16},{16,0},{32,48},{48,32},{64,80},{80,64},{96,112},{112,96},{1... | collective-permute-start | bytes 1179656 | tf_op jit(solution)/shard_map/ppermute | solution.py:187
  12.4 32.6 %copy-start.2 = (f32[3,32,16]{1,2,0:T(8,128)S(1)}, f32[3,32,16]{1,2,0:T(8,128)}, u32[]{:S(2)}) copy-start(f32[3,32,16]{1,2,0:T(8,128)} %param.9) | copy-start | bytes 18436
  45.0 42.6 %copy-start.1 = (f32[3,32,1792]{2,1,0:T(8,128)S(1)}, f32[3,32,1792]{2,1,0:T(8,128)}, u32[]{:S(2)}) copy-start(f32[3,32,1792]{2,1,0:T(8,128)} %refs_5_.1) | copy-start | bytes 2064388
  58.6 29.1 %copy-start = (bf16[3,32,1792]{2,1,0:T(8,128)(2,1)S(1)}, bf16[3,32,1792]{2,1,0:T(8,128)(2,1)}, u32[]{:S(2)}) copy-start(bf16[3,32,1792]{2,1,0:T(8,128)(2,1)} %refs_4_.1) | copy-start | bytes 1032196
  79.3 8.3 %collective-permute-start.1 = (f32[16,32,128]{2,1,0:T(8,128)S(1)}, f32[16,32,128]{2,1,0:T(8,128)S(1)}, u32[]{:S(2)}, u32[]{:S(2)}) collective-permute-start(f32[16,32,128]{2,1,0:T(8,128)S(1)} %all_to_all.17.refs_2_), channel_id=1, source_target_pairs={{0,16},{16,0},{32,48},{48,32},{64,80},{80,64},{96,112},{112,96},{1... | collective-permute-start | bytes 786440 | tf_op jit(solution)/shard_map/ppermute | solution.py:187
where the time goes:
time: 91.8 us; the launch traced here: 91.5 us
  blocking collectives  66.4 us (72%)
  starting transfers between devices  16 us (17%)
  Pallas kernels  5.88 us (6%)
  waiting for transfers between devices  2.47 us (3%)
    all_to_all x2, blocking collectives, exchange_z(): lax.all_to_all(x, 'replica', 0, 0, axis_index_groups=groups, tiled=True)  53.3 us
    ppermute x2, starting transfers between devices, sibling(): return lax.ppermute(x, 'replica', [(i, i ^ 1) for i in range(2 * CHIPS)])  16 us
    all_to_all x1, blocking collectives, local(): lax.all_to_all(jnp.broadcast_to(inner, (16, MROWS, BLOCK)), 'fsdp', 0, 0,...  13.1 us
    pallas_call x1, Pallas kernels, local(): pl.pallas_call(lambda *refs: final_kernel(lax.axis_size('replica'), *refs...  3.81 us
    ppermute x2, waiting for transfers between devices, sibling(): return lax.ppermute(x, 'replica', [(i, i ^ 1) for i in range(2 * CHIPS)])  2.47 us
  transfers between devices with their start and end apart: 2, of which 2 were waited for; matrix products, arithmetic and copies ran while one was open for 0% of the time, Pallas kernels for 0%

commit v1 on v0

--- a/solution.py
+++ b/solution.py
@@ -121,8 +121,8 @@
 ):
     first = ids[0] == 0
 
-    mine = jnp.sum(own[:, FROWS:GROWS], axis=0)
-    other = jnp.sum(sib[:, FROWS:GROWS], axis=0)
+    rows = slice(CHIPS * FROWS, CHIPS * FROWS + MROWS)
+    mine, other = own[rows], sib[rows]
     middle = pltpu.roll(mine + other, SIDE, 1)
     table = []
     for mat, rows in enumerate(
@@ -147,8 +147,8 @@
     left = left_side(8)
     for block in range(BLOCKS):
         lanes = slice(block * BLOCK, (block + 1) * BLOCK)
-        mine = own[slot_of(block, ids[0]), 0:FROWS]
-        other = sib[slot_of(block, 1 - ids[0]), 0:FROWS]
+        mine = own[pl.ds(pl.multiple_of(slot_of(block, ids[0]) * FROWS, 8), FROWS)]
+        other = sib[pl.ds(pl.multiple_of(slot_of(block, 1 - ids[0]) * FROWS, 8), FROWS)]
         low, high = jnp.where(first, mine, other), jnp.where(first, other, mine)
         low_half, high_half = low[RANK:FROWS], high[RANK:FROWS]
         half = jnp.concatenate(
@@ -192,6 +192,19 @@
     return lax.all_to_all(x, "replica", 0, 0, axis_index_groups=groups, tiled=True)
 
 
+def exchange_mixed(x, line_core):
+    lines = [
+        [(2 * chip_at(slot, line_core) + line_core) * 16 + place for slot in range(CHIPS)]
+        for place in range(16)
+    ]
+    planes = [
+        [(2 * chip + 1 - line_core) * 16 + place for place in range(16)] for chip in range(CHIPS)
+    ]
+    return lax.all_to_all(
+        x, ("replica", "fsdp"), 0, 0, axis_index_groups=lines + planes, tiled=True
+    )
+
+
 def local(weights, local_weights, carried_error, momentum, initial_factor):
     f32 = jnp.float32
     ids = (lax.axis_index("replica") & 1).astype(jnp.int32).reshape(1)
@@ -224,13 +237,15 @@
         name="factor",
     )(ids, qt, shares)
 
-    inner = lax.all_to_all(
-        jnp.broadcast_to(inner, (16, MROWS, BLOCK)), "fsdp", 0, 0, tiled=True
-    )
-    inner = jnp.sum(inner, axis=0)
-    own = exchange_z(
-        jnp.broadcast_to(jnp.concatenate([factor, inner]), (CHIPS, GROWS, BLOCK))
-    )
+    factors = []
+    for line_core in (1, 0):
+        rows = exchange_mixed(
+            jnp.broadcast_to(jnp.concatenate([factor, inner]), (CHIPS, GROWS, BLOCK)), line_core
+        )
+        factors.append(rows[:, :FROWS])
+        inner = jnp.sum(rows[:, FROWS:], axis=0)
+    factors = jnp.where(ids[0] == 0, factors[1], factors[0])
+    own = jnp.concatenate([factors.reshape(CHIPS * FROWS, BLOCK), inner])
     sib = sibling(own)
 
     next_weights, next_error, next_momentum, following = pl.pallas_call(

time: 91.8 us -> 93.8 us (1.022)
  blocking collectives: 66.4 us -> 50.3 us
  starting transfers between devices: 16 us -> 25.4 us
  waiting for transfers between devices: 2.47 us -> 10.2 us
    all_to_all x2 -> x1, blocking collectives: 53.3 us -> 32.6 us  [exchange_z(): lax.all_to_all(x, 'replica', 0, 0, axis_index_groups=groups, tiled=True)]
    all_to_all x0 -> x1, waiting for transfers between devices: none -> 7.83 us  [exchange_mixed(): lax.all_to_all(x, ('replica', 'fsdp'), 0, 0, axis_index_groups=lines + pl...]
    all_to_all x0 -> x1, starting transfers between devices: none -> 6.89 us  [exchange_mixed(): lax.all_to_all(x, ('replica', 'fsdp'), 0, 0, axis_index_groups=lines + pl...]
    all_to_all x1, blocking collectives: 13.1 us -> 17.7 us  [exchange_mixed(): lax.all_to_all(x, ('replica', 'fsdp'), 0, 0, axis_index_groups=lines + pl...]
    ppermute x2, starting transfers between devices: 16 us -> 18.6 us  [sibling(): return lax.ppermute(x, 'replica', [(i, i ^ 1) for i in range(2 * CHIPS)])]
  transfers between devices with their start and end apart: 2 -> 3, of which waited for: 2 -> 3; matrix products, arithmetic and copies ran while one was open for 0% -> 0% of each run, Pallas kernels for 0% -> 0%
where the time goes in v1:
time: 93.8 us; the launch traced here: 93.4 us
  blocking collectives  50.3 us (54%)
  starting transfers between devices  25.4 us (27%)
  waiting for transfers between devices  10.2 us (11%)
  Pallas kernels  5.85 us (6%)
    all_to_all x1, blocking collectives, exchange_z(): lax.all_to_all(x, 'replica', 0, 0, axis_index_groups=groups, tiled=True)  32.6 us
    ppermute x2, starting transfers between devices, sibling(): return lax.ppermute(x, 'replica', [(i, i ^ 1) for i in range(2 * CHIPS)])  18.6 us
    all_to_all x1, blocking collectives, exchange_mixed(): lax.all_to_all(x, ('replica', 'fsdp'), 0, 0, axis_index_groups=lines + pl...  17.7 us
    all_to_all x1, waiting for transfers between devices, exchange_mixed(): lax.all_to_all(x, ('replica', 'fsdp'), 0, 0, axis_index_groups=lines + pl...  7.83 us
    all_to_all x1, starting transfers between devices, exchange_mixed(): lax.all_to_all(x, ('replica', 'fsdp'), 0, 0, axis_index_groups=lines + pl...  6.89 us
    pallas_call x1, Pallas kernels, local(): pl.pallas_call(lambda *refs: final_kernel(lax.axis_size('replica'), *refs...  3.78 us
    ppermute x2, waiting for transfers between devices, sibling(): return lax.ppermute(x, 'replica', [(i, i ^ 1) for i in range(2 * CHIPS)])  2.38 us
  transfers between devices with their start and end apart: 3, of which 3 were waited for; matrix products, arithmetic and copies ran while one was open for 0% of the time, Pallas kernels for 0%

profile of v1, /device:TPU:1, one launch (start us, length us, event | category | flops | bytes accessed | tf_op | source)
XLA Modules:
  0.0 93.4 jit_solution(7144630924463499769)
XLA Ops:
  0.6 1.6 %pack.1 = (f32[16,48,128]{2,1,0:T(8,128)S(1)}, f32[16,48,128]{2,1,0:T(8,128)S(1)}, f32[3,32,1792]{2,1,0:T(8,128)S(1)}) custom-call(s32[1]{0:T(128)} %bitcast.ids.refs_0_, bf16[3,32,1792]{2,1,0:T(8,128)(2,1)} %refs_4_.1, bf16[3,32,1792]{2,1,0:T(8,128)(2,1)} %bitcast.11, f32[3,32,1792]{2,1,0:T(8,128)} %bitcast.10), custom_call_target="tpu_custom_call" | custom-call | tf_op jit(solution)/shard_map/pack/pallas_call | solution.py:212
  2.3 8.8 %collective-permute-start = (f32[16,48,128]{2,1,0:T(8,128)S(1)}, f32[16,48,128]{2,1,0:T(8,128)S(1)}, u32[]{:S(2)}, u32[]{:S(2)}) collective-permute-start(f32[16,48,128]{2,1,0:T(8,128)S(1)} %get-tuple-element.14), channel_id=1, source_target_pairs={{0,16},{16,0},{32,48},{48,32},{64,80},{80,64},{96,112},{112,96},{1... | collective-permute-start | bytes 1179656 | tf_op jit(solution)/shard_map/ppermute | solution.py:187
  11.1 1.3 %collective-permute-done = f32[16,48,128]{2,1,0:T(8,128)S(1)} collective-permute-done((f32[16,48,128]{2,1,0:T(8,128)S(1)}, f32[16,48,128]{2,1,0:T(8,128)S(1)}, u32[]{:S(2)}, u32[]{:S(2)}) %collective-permute-start) | collective-permute-done | bytes 393248 | tf_op jit(solution)/shard_map/ppermute | solution.py:187
  12.4 0.0 copy-start.2
  12.5 32.6 %all_to_all.15.got = f32[16,48,128]{2,1,0:T(8,128)S(1)} all-to-all(f32[16,48,128]{2,1,0:T(8,128)S(1)} %add.3), channel_id=1, replica_groups={{0,256,128,384,64,320,192,448,32,288,160,416,96,352,224,480},{400,144,2..., dimensions={0} | all-to-all | bytes 786432 | tf_op jit(solution)/shard_map/all_to_all | solution.py:192
  45.0 0.0 copy-done.2
  45.0 0.4 factor.1
  45.5 0.1 broadcast_in_dim.9
  45.5 17.7 %all_to_all.16 = f32[16,32,128]{2,1,0:T(8,128)S(1)} all-to-all(f32[16,32,128]{2,1,0:T(8,128)S(1)} %broadcast_in_dim.9), channel_id=1, replica_groups={{400,144,272,16,464,208,336,80,432,176,304,48,496,240,368,112},{401,145..., dimensions={0} | all-to-all | bytes 524288 | tf_op jit(solution)/shard_map/all_to_all | solution.py:203
  63.3 0.7 broadcast_in_dim.10
  64.0 0.0 copy-start.1
  64.0 6.9 %all-to-all-start.2 = ((f32[16,32,128]{2,1,0:T(8,128)}), f32[16,32,128]{2,1,0:T(8,128)S(1)}, u32[]{:S(2)}, u32[]{:S(2)}) async-start(f32[16,32,128]{2,1,0:T(8,128)} %broadcast_in_dim.10), calls=%async_computation.2 | async-start | bytes 524288 | tf_op jit(solution)/shard_map/all_to_all | solution.py:203
  70.9 7.8 %all-to-all-done.2 = f32[16,32,128]{2,1,0:T(8,128)S(1)} async-done(((f32[16,32,128]{2,1,0:T(8,128)}), f32[16,32,128]{2,1,0:T(8,128)S(1)}, u32[]{:S(2)}, u32[]{:S(2)}) %all-to-all-start.2) | async-done | bytes 262176 | tf_op jit(solution)/shard_map/all_to_all | solution.py:203
  78.8 0.0 copy-start
  78.8 9.8 %collective-permute-start.1 = (f32[392,128]{1,0:T(8,128)S(1)}, f32[392,128]{1,0:T(8,128)S(1)}, u32[]{:S(2)}, u32[]{:S(2)}) collective-permute-start(f32[392,128]{1,0:T(8,128)S(1)} %pad_maximum_fusion.refs_2_), channel_id=1, source_target_pairs={{0,16},{16,0},{32,48},{48,32},{64,80},{80,64},{96,112},{112,96},{1... | collective-permute-start | bytes 602120 | tf_op jit(solution)/shard_map/ppermute | solution.py:187
  88.6 1.1 %collective-permute-done.1.refs_3_ = f32[392,128]{1,0:T(8,128)S(1)} collective-permute-done((f32[392,128]{1,0:T(8,128)S(1)}, f32[392,128]{1,0:T(8,128)S(1)}, u32[]{:S(2)}, u32[]{:S(2)}) %collective-permute-start.1) | collective-permute-done | bytes 200736 | tf_op jit(solution)/shard_map/ppermute | solution.py:187
  89.6 0.0 copy-done.1
  89.6 0.0 copy-done
  89.7 3.8 %final.1 = (bf16[3,32,1792]{2,1,0:T(8,128)(2,1)}, f32[3,32,1792]{2,1,0:T(8,128)}, f32[3,32,1792]{2,1,0:T(8,128)}, f32[3,16,32]{2,1,0:T(8,128)}) custom-call(s32[1]{0:T(128)} %bitcast.ids.refs_0_, f32[3,16,32]{2,1,0:T(8,128)S(1)} %bitcast.8, f32[392,128]{1,0:T(8,128)S(1)} %pad_maximum_fusion.refs_2_, f32[392,128]{1,0:T(8,128)S(1)} %collective-permute-done.1.refs_3_, ...), custom_call_target="tpu_custom_call" | custom-call | tf_op jit(solution)/shard_map/final/pallas_call | solution.py:251
  (7 shorter events, 0.1 us)
Async XLA Ops:
  2.3 10.1 %collective-permute-start = (f32[16,48,128]{2,1,0:T(8,128)S(1)}, f32[16,48,128]{2,1,0:T(8,128)S(1)}, u32[]{:S(2)}, u32[]{:S(2)}) collective-permute-start(f32[16,48,128]{2,1,0:T(8,128)S(1)} %get-tuple-element.14), channel_id=1, source_target_pairs={{0,16},{16,0},{32,48},{48,32},{64,80},{80,64},{96,112},{112,96},{1... | collective-permute-start | bytes 1179656 | tf_op jit(solution)/shard_map/ppermute | solution.py:187
  12.4 32.6 %copy-start.2 = (f32[3,32,16]{1,2,0:T(8,128)S(1)}, f32[3,32,16]{1,2,0:T(8,128)}, u32[]{:S(2)}) copy-start(f32[3,32,16]{1,2,0:T(8,128)} %param.9) | copy-start | bytes 18436
  64.0 25.7 %copy-start.1 = (f32[3,32,1792]{2,1,0:T(8,128)S(1)}, f32[3,32,1792]{2,1,0:T(8,128)}, u32[]{:S(2)}) copy-start(f32[3,32,1792]{2,1,0:T(8,128)} %refs_5_.1) | copy-start | bytes 2064388
  64.0 14.7 %all-to-all-start.2 = ((f32[16,32,128]{2,1,0:T(8,128)}), f32[16,32,128]{2,1,0:T(8,128)S(1)}, u32[]{:S(2)}, u32[]{:S(2)}) async-start(f32[16,32,128]{2,1,0:T(8,128)} %broadcast_in_dim.10), calls=%async_computation.2 | async-start | bytes 524288 | tf_op jit(solution)/shard_map/all_to_all | solution.py:203
  78.8 10.9 %copy-start = (bf16[3,32,1792]{2,1,0:T(8,128)(2,1)S(1)}, bf16[3,32,1792]{2,1,0:T(8,128)(2,1)}, u32[]{:S(2)}) copy-start(bf16[3,32,1792]{2,1,0:T(8,128)(2,1)} %refs_4_.1) | copy-start | bytes 1032196
  78.8 10.8 %collective-permute-start.1 = (f32[392,128]{1,0:T(8,128)S(1)}, f32[392,128]{1,0:T(8,128)S(1)}, u32[]{:S(2)}, u32[]{:S(2)}) collective-permute-start(f32[392,128]{1,0:T(8,128)S(1)} %pad_maximum_fusion.refs_2_), channel_id=1, source_target_pairs={{0,16},{16,0},{32,48},{48,32},{64,80},{80,64},{96,112},{112,96},{1... | collective-permute-start | bytes 602120 | tf_op jit(solution)/shard_map/ppermute | solution.py:187

commit v2 on v1

--- a/solution.py
+++ b/solution.py
@@ -108,6 +108,16 @@
     inner[...] = jnp.concatenate([whole[0:8], whole[8:16], half[0:8], half[8:16]], axis=1)
 
 
+def choose_kernel(ids, one, two, out):
+    out[CHIPS * FROWS :] = jnp.sum(two[:, FROWS:GROWS], axis=0)
+    for core, arrived in enumerate((two, one)):
+
+        @pl.when(ids[0] == core)
+        def _():
+            for slot in range(CHIPS):
+                out[slot * FROWS : slot * FROWS + FROWS] = arrived[slot, 0:FROWS]
+
+
 def split(x):
     high = x.astype(jnp.bfloat16)
     rest = x - high.astype(jnp.float32)
@@ -237,15 +247,23 @@
         name="factor",
     )(ids, qt, shares)
 
-    factors = []
+    arrivals = []
     for line_core in (1, 0):
-        rows = exchange_mixed(
-            jnp.broadcast_to(jnp.concatenate([factor, inner]), (CHIPS, GROWS, BLOCK)), line_core
+        arrivals.append(
+            exchange_mixed(
+                jnp.broadcast_to(jnp.concatenate([factor, inner]), (CHIPS, GROWS, BLOCK)),
+                line_core,
+            )
         )
-        factors.append(rows[:, :FROWS])
-        inner = jnp.sum(rows[:, FROWS:], axis=0)
-    factors = jnp.where(ids[0] == 0, factors[1], factors[0])
-    own = jnp.concatenate([factors.reshape(CHIPS * FROWS, BLOCK), inner])
+        inner = jnp.sum(arrivals[-1][:, FROWS:], axis=0)
+    own = pl.pallas_call(
+        choose_kernel,
+        out_shape=pltpu.VMEM((CHIPS * FROWS + MROWS, BLOCK), f32),
+        in_specs=[SMEM, VMEM, VMEM],
+        out_specs=VMEM,
+        compiler_params=PARAMS,
+        name="choose",
+    )(ids, *arrivals)
     sib = sibling(own)
 
     next_weights, next_error, next_momentum, following = pl.pallas_call(

time: 93.8 us -> 92.8 us (0.989)
  blocking collectives: 50.3 us -> 64.8 us
  waiting for transfers between devices: 10.2 us -> 2.38 us
  starting transfers between devices: 25.4 us -> 18.5 us
    all_to_all x1 -> x2, blocking collectives: 17.7 us -> 32.2 us  [exchange_mixed(): lax.all_to_all(x, ('replica', 'fsdp'), 0, 0, axis_index_groups=lines + pl...]
    all_to_all x1 -> x0, waiting for transfers between devices: 7.83 us -> none  [exchange_mixed(): lax.all_to_all(x, ('replica', 'fsdp'), 0, 0, axis_index_groups=lines + pl...]
    all_to_all x1 -> x0, starting transfers between devices: 6.89 us -> none  [exchange_mixed(): lax.all_to_all(x, ('replica', 'fsdp'), 0, 0, axis_index_groups=lines + pl...]
  transfers between devices with their start and end apart: 3 -> 2, of which waited for: 3 -> 2; matrix products, arithmetic and copies ran while one was open for 0% -> 0% of each run, Pallas kernels for 0% -> 0%
where the time goes in v2:
time: 92.8 us; the launch traced here: 92.5 us
  blocking collectives  64.8 us (70%)
  starting transfers between devices  18.5 us (20%)
  Pallas kernels  5.89 us (6%)
  waiting for transfers between devices  2.38 us (3%)
    all_to_all x1, blocking collectives, exchange_z(): lax.all_to_all(x, 'replica', 0, 0, axis_index_groups=groups, tiled=True)  32.6 us
    all_to_all x2, blocking collectives, exchange_mixed(): lax.all_to_all(x, ('replica', 'fsdp'), 0, 0, axis_index_groups=lines + pl...  32.2 us
    ppermute x2, starting transfers between devices, sibling(): return lax.ppermute(x, 'replica', [(i, i ^ 1) for i in range(2 * CHIPS)])  18.5 us
    pallas_call x1, Pallas kernels, local(): pl.pallas_call(lambda *refs: final_kernel(lax.axis_size('replica'), *refs...  3.79 us
    ppermute x2, waiting for transfers between devices, sibling(): return lax.ppermute(x, 'replica', [(i, i ^ 1) for i in range(2 * CHIPS)])  2.38 us
  transfers between devices with their start and end apart: 2, of which 2 were waited for; matrix products, arithmetic and copies ran while one was open for 0% of the time, Pallas kernels for 0%

profile of v2, /device:TPU:1, one launch (start us, length us, event | category | flops | bytes accessed | tf_op | source)
XLA Modules:
  0.0 92.5 jit_solution(18092489530975655956)
XLA Ops:
  0.6 1.6 %pack.1 = (f32[16,48,128]{2,1,0:T(8,128)S(1)}, f32[16,48,128]{2,1,0:T(8,128)S(1)}, f32[3,32,1792]{2,1,0:T(8,128)S(1)}) custom-call(s32[1]{0:T(128)} %bitcast.ids.refs_0_, bf16[3,32,1792]{2,1,0:T(8,128)(2,1)} %refs_4_.1, bf16[3,32,1792]{2,1,0:T(8,128)(2,1)} %bitcast.9, f32[3,32,1792]{2,1,0:T(8,128)} %bitcast.8), custom_call_target="tpu_custom_call" | custom-call | tf_op jit(solution)/shard_map/pack/pallas_call | solution.py:222
  2.3 8.8 %collective-permute-start = (f32[16,48,128]{2,1,0:T(8,128)S(1)}, f32[16,48,128]{2,1,0:T(8,128)S(1)}, u32[]{:S(2)}, u32[]{:S(2)}) collective-permute-start(f32[16,48,128]{2,1,0:T(8,128)S(1)} %get-tuple-element.14), channel_id=1, source_target_pairs={{0,16},{16,0},{32,48},{48,32},{64,80},{80,64},{96,112},{112,96},{1... | collective-permute-start | bytes 1179656 | tf_op jit(solution)/shard_map/ppermute | solution.py:197
  11.1 1.3 %collective-permute-done = f32[16,48,128]{2,1,0:T(8,128)S(1)} collective-permute-done((f32[16,48,128]{2,1,0:T(8,128)S(1)}, f32[16,48,128]{2,1,0:T(8,128)S(1)}, u32[]{:S(2)}, u32[]{:S(2)}) %collective-permute-start) | collective-permute-done | bytes 393248 | tf_op jit(solution)/shard_map/ppermute | solution.py:197
  12.4 0.1 add.3
  12.5 0.0 copy-start.2
  12.5 32.6 %all_to_all.15.got = f32[16,48,128]{2,1,0:T(8,128)S(1)} all-to-all(f32[16,48,128]{2,1,0:T(8,128)S(1)} %add.3), channel_id=1, replica_groups={{0,256,128,384,64,320,192,448,32,288,160,416,96,352,224,480},{400,144,2..., dimensions={0} | all-to-all | bytes 786432 | tf_op jit(solution)/shard_map/all_to_all | solution.py:202
  45.0 0.0 copy-done.2
  45.0 0.4 factor.1
  45.5 0.1 broadcast_in_dim.9
  45.5 17.7 %all_to_all.16.one = f32[16,32,128]{2,1,0:T(8,128)S(1)} all-to-all(f32[16,32,128]{2,1,0:T(8,128)S(1)} %broadcast_in_dim.9), channel_id=1, replica_groups={{400,144,272,16,464,208,336,80,432,176,304,48,496,240,368,112},{401,145..., dimensions={0} | all-to-all | bytes 524288 | tf_op jit(solution)/shard_map/all_to_all | solution.py:213
  63.3 0.0 copy-start.1
  63.3 14.5 %all_to_all.17.two = f32[16,32,128]{2,1,0:T(8,128)S(1)} all-to-all(f32[16,32,128]{2,1,0:T(8,128)S(1)} %broadcast_in_dim.10), channel_id=1, replica_groups={{0,256,128,384,64,320,192,448,32,288,160,416,96,352,224,480},{1,257,129..., dimensions={0} | all-to-all | bytes 524288 | tf_op jit(solution)/shard_map/all_to_all | solution.py:213
  77.8 0.0 copy-start
  77.9 9.8 %collective-permute-start.1 = (f32[392,128]{1,0:T(8,128)S(1)}, f32[392,128]{1,0:T(8,128)S(1)}, u32[]{:S(2)}, u32[]{:S(2)}) collective-permute-start(f32[392,128]{1,0:T(8,128)S(1)} %choose.1.refs_2_), channel_id=1, source_target_pairs={{0,16},{16,0},{32,48},{48,32},{64,80},{80,64},{96,112},{112,96},{1... | collective-permute-start | bytes 602120 | tf_op jit(solution)/shard_map/ppermute | solution.py:197
  87.6 1.1 %collective-permute-done.1.refs_3_ = f32[392,128]{1,0:T(8,128)S(1)} collective-permute-done((f32[392,128]{1,0:T(8,128)S(1)}, f32[392,128]{1,0:T(8,128)S(1)}, u32[]{:S(2)}, u32[]{:S(2)}) %collective-permute-start.1) | collective-permute-done | bytes 200736 | tf_op jit(solution)/shard_map/ppermute | solution.py:197
  88.7 0.0 copy-done.1
  88.7 0.0 copy-done
  88.7 3.8 %final.1 = (bf16[3,32,1792]{2,1,0:T(8,128)(2,1)}, f32[3,32,1792]{2,1,0:T(8,128)}, f32[3,32,1792]{2,1,0:T(8,128)}, f32[3,16,32]{2,1,0:T(8,128)}) custom-call(s32[1]{0:T(128)} %bitcast.ids.refs_0_, f32[3,16,32]{2,1,0:T(8,128)S(1)} %bitcast.7, f32[392,128]{1,0:T(8,128)S(1)} %choose.1.refs_2_, f32[392,128]{1,0:T(8,128)S(1)} %collective-permute-done.1.refs_3_, ...), custom_call_target="tpu_custom_call" | custom-call | tf_op jit(solution)/shard_map/final/pallas_call | solution.py:269
  (5 shorter events, 0.1 us)
Async XLA Ops:
  2.3 10.1 %collective-permute-start = (f32[16,48,128]{2,1,0:T(8,128)S(1)}, f32[16,48,128]{2,1,0:T(8,128)S(1)}, u32[]{:S(2)}, u32[]{:S(2)}) collective-permute-start(f32[16,48,128]{2,1,0:T(8,128)S(1)} %get-tuple-element.14), channel_id=1, source_target_pairs={{0,16},{16,0},{32,48},{48,32},{64,80},{80,64},{96,112},{112,96},{1... | collective-permute-start | bytes 1179656 | tf_op jit(solution)/shard_map/ppermute | solution.py:197
  12.5 32.6 %copy-start.2 = (f32[3,32,16]{1,2,0:T(8,128)S(1)}, f32[3,32,16]{1,2,0:T(8,128)}, u32[]{:S(2)}) copy-start(f32[3,32,16]{1,2,0:T(8,128)} %param.9) | copy-start | bytes 18436
  63.3 25.4 %copy-start.1 = (f32[3,32,1792]{2,1,0:T(8,128)S(1)}, f32[3,32,1792]{2,1,0:T(8,128)}, u32[]{:S(2)}) copy-start(f32[3,32,1792]{2,1,0:T(8,128)} %refs_5_.1) | copy-start | bytes 2064388
  77.8 10.9 %copy-start = (bf16[3,32,1792]{2,1,0:T(8,128)(2,1)S(1)}, bf16[3,32,1792]{2,1,0:T(8,128)(2,1)}, u32[]{:S(2)}) copy-start(bf16[3,32,1792]{2,1,0:T(8,128)(2,1)} %refs_4_.1) | copy-start | bytes 1032196
  77.9 10.8 %collective-permute-start.1 = (f32[392,128]{1,0:T(8,128)S(1)}, f32[392,128]{1,0:T(8,128)S(1)}, u32[]{:S(2)}, u32[]{:S(2)}) collective-permute-start(f32[392,128]{1,0:T(8,128)S(1)} %choose.1.refs_2_), channel_id=1, source_target_pairs={{0,16},{16,0},{32,48},{48,32},{64,80},{80,64},{96,112},{112,96},{1... | collective-permute-start | bytes 602120 | tf_op jit(solution)/shard_map/ppermute | solution.py:197

commit v3 on v2

--- a/solution.py
+++ b/solution.py
@@ -26,15 +26,12 @@
 PACK_PARAMS = pltpu.CompilerParams(vmem_limit_bytes=56 * 1024 * 1024)
 
 
-REVERSED = [int(format(i, "04b")[::-1], 2) for i in range(CHIPS)]
-
-
 def slot_of(chip, core):
-    return REVERSED[chip] ^ (3 * core)
+    return chip ^ ((CHIPS - 1) * core)
 
 
 def chip_at(slot, core):
-    return REVERSED[slot ^ (3 * core)]
+    return slot ^ ((CHIPS - 1) * core)
 
 
 def swap_sides(x):

time: 92.8 us -> 89.7 us (0.967)
  starting transfers between devices: 18.5 us -> 13.5 us
  blocking collectives: 64.8 us -> 66.7 us
    ppermute x2, starting transfers between devices: 18.5 us -> 13.5 us  [sibling(): return lax.ppermute(x, 'replica', [(i, i ^ 1) for i in range(2 * CHIPS)])]
    all_to_all x2, blocking collectives: 32.2 us -> 34.9 us  [exchange_mixed(): lax.all_to_all(x, ('replica', 'fsdp'), 0, 0, axis_index_groups=lines + pl...]
where the time goes in v3:
time: 89.7 us; the launch traced here: 89.3 us
  blocking collectives  66.7 us (74%)
  starting transfers between devices  13.5 us (15%)
  Pallas kernels  5.89 us (7%)
  waiting for transfers between devices  2.38 us (3%)
    all_to_all x2, blocking collectives, exchange_mixed(): lax.all_to_all(x, ('replica', 'fsdp'), 0, 0, axis_index_groups=lines + pl...  34.9 us
    all_to_all x1, blocking collectives, exchange_z(): lax.all_to_all(x, 'replica', 0, 0, axis_index_groups=groups, tiled=True)  31.8 us
    ppermute x2, starting transfers between devices, sibling(): return lax.ppermute(x, 'replica', [(i, i ^ 1) for i in range(2 * CHIPS)])  13.5 us
    pallas_call x1, Pallas kernels, local(): pl.pallas_call(lambda *refs: final_kernel(lax.axis_size('replica'), *refs...  3.79 us
    ppermute x2, waiting for transfers between devices, sibling(): return lax.ppermute(x, 'replica', [(i, i ^ 1) for i in range(2 * CHIPS)])  2.38 us
  transfers between devices with their start and end apart: 2, of which 2 were waited for; matrix products, arithmetic and copies ran while one was open for 0% of the time, Pallas kernels for 0%

profile of v3, /device:TPU:1, one launch (start us, length us, event | category | flops | bytes accessed | tf_op | source)
XLA Modules:
  0.0 89.3 jit_solution(2155249951772704993)
XLA Ops:
  0.6 1.6 %pack.1 = (f32[16,48,128]{2,1,0:T(8,128)S(1)}, f32[16,48,128]{2,1,0:T(8,128)S(1)}, f32[3,32,1792]{2,1,0:T(8,128)S(1)}) custom-call(s32[1]{0:T(128)} %bitcast.ids.refs_0_, bf16[3,32,1792]{2,1,0:T(8,128)(2,1)} %refs_4_.1, bf16[3,32,1792]{2,1,0:T(8,128)(2,1)} %bitcast.9, f32[3,32,1792]{2,1,0:T(8,128)} %bitcast.8), custom_call_target="tpu_custom_call" | custom-call | tf_op jit(solution)/shard_map/pack/pallas_call | solution.py:219
  2.3 8.8 %collective-permute-start = (f32[16,48,128]{2,1,0:T(8,128)S(1)}, f32[16,48,128]{2,1,0:T(8,128)S(1)}, u32[]{:S(2)}, u32[]{:S(2)}) collective-permute-start(f32[16,48,128]{2,1,0:T(8,128)S(1)} %get-tuple-element.14), channel_id=1, source_target_pairs={{0,16},{16,0},{32,48},{48,32},{64,80},{80,64},{96,112},{112,96},{1... | collective-permute-start | bytes 1179656 | tf_op jit(solution)/shard_map/ppermute | solution.py:194
  11.1 1.3 %collective-permute-done = f32[16,48,128]{2,1,0:T(8,128)S(1)} collective-permute-done((f32[16,48,128]{2,1,0:T(8,128)S(1)}, f32[16,48,128]{2,1,0:T(8,128)S(1)}, u32[]{:S(2)}, u32[]{:S(2)}) %collective-permute-start) | collective-permute-done | bytes 393248 | tf_op jit(solution)/shard_map/ppermute | solution.py:194
  12.4 0.1 add.3
  12.5 0.0 copy-start.2
  12.5 31.8 %all_to_all.15.got = f32[16,48,128]{2,1,0:T(8,128)S(1)} all-to-all(f32[16,48,128]{2,1,0:T(8,128)S(1)} %add.3), channel_id=1, replica_groups={{0,32,64,96,128,160,192,224,256,288,320,352,384,416,448,480},{496,464,4..., dimensions={0} | all-to-all | bytes 786432 | tf_op jit(solution)/shard_map/all_to_all | solution.py:199
  44.2 0.0 copy-done.2
  44.2 0.4 factor.1
  44.7 0.1 broadcast_in_dim.9
  44.7 20.4 %all_to_all.16.one = f32[16,32,128]{2,1,0:T(8,128)S(1)} all-to-all(f32[16,32,128]{2,1,0:T(8,128)S(1)} %broadcast_in_dim.9), channel_id=1, replica_groups={{496,464,432,400,368,336,304,272,240,208,176,144,112,80,48,16},{497,465..., dimensions={0} | all-to-all | bytes 524288 | tf_op jit(solution)/shard_map/all_to_all | solution.py:210
  65.2 0.0 copy-start.1
  65.2 14.5 %all_to_all.17.two = f32[16,32,128]{2,1,0:T(8,128)S(1)} all-to-all(f32[16,32,128]{2,1,0:T(8,128)S(1)} %broadcast_in_dim.10), channel_id=1, replica_groups={{0,32,64,96,128,160,192,224,256,288,320,352,384,416,448,480},{1,33,65,9..., dimensions={0} | all-to-all | bytes 524288 | tf_op jit(solution)/shard_map/all_to_all | solution.py:210
  79.7 0.0 copy-start
  79.7 4.7 %collective-permute-start.1 = (f32[392,128]{1,0:T(8,128)S(1)}, f32[392,128]{1,0:T(8,128)S(1)}, u32[]{:S(2)}, u32[]{:S(2)}) collective-permute-start(f32[392,128]{1,0:T(8,128)S(1)} %choose.1.refs_2_), channel_id=1, source_target_pairs={{0,16},{16,0},{32,48},{48,32},{64,80},{80,64},{96,112},{112,96},{1... | collective-permute-start | bytes 602120 | tf_op jit(solution)/shard_map/ppermute | solution.py:194
  84.5 1.1 %collective-permute-done.1.refs_3_ = f32[392,128]{1,0:T(8,128)S(1)} collective-permute-done((f32[392,128]{1,0:T(8,128)S(1)}, f32[392,128]{1,0:T(8,128)S(1)}, u32[]{:S(2)}, u32[]{:S(2)}) %collective-permute-start.1) | collective-permute-done | bytes 200736 | tf_op jit(solution)/shard_map/ppermute | solution.py:194
  85.5 0.0 copy-done.1
  85.5 0.0 copy-done
  85.5 3.8 %final.1 = (bf16[3,32,1792]{2,1,0:T(8,128)(2,1)}, f32[3,32,1792]{2,1,0:T(8,128)}, f32[3,32,1792]{2,1,0:T(8,128)}, f32[3,16,32]{2,1,0:T(8,128)}) custom-call(s32[1]{0:T(128)} %bitcast.ids.refs_0_, f32[3,16,32]{2,1,0:T(8,128)S(1)} %bitcast.7, f32[392,128]{1,0:T(8,128)S(1)} %choose.1.refs_2_, f32[392,128]{1,0:T(8,128)S(1)} %collective-permute-done.1.refs_3_, ...), custom_call_target="tpu_custom_call" | custom-call | tf_op jit(solution)/shard_map/final/pallas_call | solution.py:266
  (5 shorter events, 0.1 us)
Async XLA Ops:
  2.3 10.1 %collective-permute-start = (f32[16,48,128]{2,1,0:T(8,128)S(1)}, f32[16,48,128]{2,1,0:T(8,128)S(1)}, u32[]{:S(2)}, u32[]{:S(2)}) collective-permute-start(f32[16,48,128]{2,1,0:T(8,128)S(1)} %get-tuple-element.14), channel_id=1, source_target_pairs={{0,16},{16,0},{32,48},{48,32},{64,80},{80,64},{96,112},{112,96},{1... | collective-permute-start | bytes 1179656 | tf_op jit(solution)/shard_map/ppermute | solution.py:194
  12.5 31.8 %copy-start.2 = (f32[3,32,16]{1,2,0:T(8,128)S(1)}, f32[3,32,16]{1,2,0:T(8,128)}, u32[]{:S(2)}) copy-start(f32[3,32,16]{1,2,0:T(8,128)} %param.9) | copy-start | bytes 18436
  65.2 20.4 %copy-start.1 = (f32[3,32,1792]{2,1,0:T(8,128)S(1)}, f32[3,32,1792]{2,1,0:T(8,128)}, u32[]{:S(2)}) copy-start(f32[3,32,1792]{2,1,0:T(8,128)} %refs_5_.1) | copy-start | bytes 2064388
  79.7 5.8 %copy-start = (bf16[3,32,1792]{2,1,0:T(8,128)(2,1)S(1)}, bf16[3,32,1792]{2,1,0:T(8,128)(2,1)}, u32[]{:S(2)}) copy-start(bf16[3,32,1792]{2,1,0:T(8,128)(2,1)} %refs_4_.1) | copy-start | bytes 1032196
  79.7 5.8 %collective-permute-start.1 = (f32[392,128]{1,0:T(8,128)S(1)}, f32[392,128]{1,0:T(8,128)S(1)}, u32[]{:S(2)}, u32[]{:S(2)}) collective-permute-start(f32[392,128]{1,0:T(8,128)S(1)} %choose.1.refs_2_), channel_id=1, source_target_pairs={{0,16},{16,0},{32,48},{48,32},{64,80},{80,64},{96,112},{112,96},{1... | collective-permute-start | bytes 602120 | tf_op jit(solution)/shard_map/ppermute | solution.py:194
